TPU v7x, 32 devices: a whole 2x2x4 slice. The times are simulated.
32 devices in a mesh: chan: 8 (over z, x), tile: 4 (over y, core).
Axes of the slice: x: 2, y: 2, z: 4, core: 2. Of those that a mesh axis runs over, the one named last changes fastest.
Arguments:
- voltages: bfloat16 [2, 1024, 5888], P(None, 'chan'), may hold values from -6 to 6
- taps: float32 [16, 256], replicated, may hold values from -0.09375 to 0.09375
- beam_weights: bfloat16 [2, 256, 64, 1024], P(None, 'chan'), may hold values from -0.1875 to 0.1875
- station_masks: int32 [64, 512], replicated, may hold values 0 or 1
- tile_pairs: int32 [36, 2], P('tile'), may hold values from 0 to 7, as said below
Outputs:
- visibilities: float32 [2, 256, 36, 128, 128], P(None, 'chan', 'tile')
- beams: bfloat16 [2, 64, 8, 256], P(None, 'tile', 'chan')
Inputs may be any that keep to these rules, and one draw needn't show every extreme that they name: `tile_pairs`: each pair (r, s) with 0 <= s <= r < 8 stands in exactly one row, r in the first column and s in the second.
All inputs are finite; a program needn't handle non-finite values.
Results may differ from a plain program's by a relative error of at most 0.0049.
Values may be sent and summed in bfloat16 or wider, within the bound.
A program may use at most 128 MiB of HBM per device.

v0:
```python
import math
import jax
import jax.numpy as jnp
from jax import lax
from jax.sharding import PartitionSpec as P

TB = 128


def dft_table(channels):
    counter = jnp.arange(channels, dtype=jnp.int32)
    wrapped = counter[:, None] * counter[None, :] % channels
    phases = 2.0 * math.pi / channels * wrapped.astype(jnp.float32)
    cosine = jnp.cos(phases)
    sine_part = jnp.sin(phases)
    first_row = jnp.stack([cosine, sine_part], axis=1)
    second_row = jnp.stack([-sine_part, cosine], axis=1)
    return jnp.stack([first_row, second_row], axis=1)


def filterbank(voltages, taps, count):
    taps_count, channels = taps.shape
    in_dev = voltages.shape[1]
    framed = voltages.reshape(2, in_dev, count + taps_count - 1, channels)
    frames = jnp.zeros((2, in_dev, count, channels), jnp.float32)
    for tap_index in range(taps_count):
        frames = frames + taps[tap_index] * framed[:, :, tap_index : tap_index + count, :].astype(
            jnp.float32
        )
    spectra = jnp.einsum(
        "crsk,sitk->crit",
        dft_table(channels),
        frames,
        precision=lax.Precision.HIGHEST,
        preferred_element_type=jnp.float32,
    )
    return spectra.astype(jnp.bfloat16)


def correlate(time_piece, tile_pairs):
    chan_dev = time_piece.shape[0]
    inputs = time_piece.shape[2]
    time_width = time_piece.shape[3]
    blocks = time_piece.reshape(chan_dev, 2, inputs // TB, TB, time_width)
    left_rows = jnp.take(blocks, tile_pairs[:, 0], axis=2)
    right_rows = jnp.take(blocks, tile_pairs[:, 1], axis=2)
    rotated = jnp.stack([left_rows[:, 1], -left_rows[:, 0]], axis=1)
    stacked = jnp.stack([left_rows, rotated], axis=0)
    return jnp.einsum(
        "ocrkaw,crkbw->ockab", stacked, right_rows, preferred_element_type=jnp.float32
    )


def beamform(own_time, beam_weights, station_masks):
    beams_count, stations = station_masks.shape
    live_inputs = jnp.broadcast_to(station_masks[:, :, None], (beams_count, stations, 2))
    live_inputs = live_inputs.reshape(beams_count, 2 * stations).astype(jnp.bfloat16)
    weights = beam_weights * live_inputs[None, None]
    products = jnp.einsum("scbi,crit->csrbt", weights, own_time, preferred_element_type=jnp.float32)
    real_part = products[:, 0, 0] - products[:, 1, 1]
    imag_part = products[:, 0, 1] + products[:, 1, 0]
    return jnp.transpose(jnp.stack([real_part, imag_part]), (0, 2, 3, 1)).astype(jnp.bfloat16)


def on_device(voltages, taps, beam_weights, station_masks, tile_pairs):
    taps_count, channels = taps.shape
    tile_count = lax.axis_size("tile")
    total_time = voltages.shape[2] // channels - taps_count + 1
    quarter = total_time // tile_count
    tile_index = lax.axis_index("tile")
    spectra = filterbank(voltages, taps, total_time)
    turned = lax.all_to_all(spectra, "chan", split_axis=0, concat_axis=2, tiled=True)
    own_time = lax.dynamic_slice_in_dim(turned, tile_index * quarter, quarter, 3)
    visibility = correlate(turned, tile_pairs)
    visibility = visibility * (1.0 / total_time)
    beam_part = beamform(own_time, beam_weights, station_masks)
    beams = lax.all_to_all(
        lax.all_to_all(beam_part, "tile", split_axis=1, concat_axis=2, tiled=True),
        "chan",
        split_axis=2,
        concat_axis=3,
        tiled=True,
    )
    return (visibility, beams)


def solution(mesh):
    in_specs = (P(None, "chan", None), P(), P(None, "chan", None, None), P(), P("tile", None))
    out_specs = (P(None, "chan", "tile", None, None), P(None, "tile", "chan", None))
    return jax.shard_map(
        on_device, mesh=mesh, in_specs=in_specs, out_specs=out_specs, check_vma=False
    )
```

profile of v0, /device:TPU:0, one launch (start us, length us, event | category | flops | bytes accessed | tf_op | source)
XLA Modules:
  0.0 124.9 jit_solution(12216933234083120169)
XLA Ops:
  0.6 1.0 fusion.109
  1.6 1.7 %fusion.107 = (f32[256,1,256]{2,0,1:T(8,128)S(1)}, f32[256,1,256]{2,0,1:T(8,128)}) fusion(), kind=kLoop, calls=%fused_computation.119 | loop fusion | flops 917504 | bytes 524288 | tf_op jit(solution)/shard_map/sin | solution.py:15
  3.3 1.7 %fusion.119 = (f32[1,256]{1,0:T(1,128)S(1)}, f32[1,256]{1,0:T(1,128)S(1)}, f32[1,256]{1,0:T(1,128)S(1)}, f32[1,256]{1,0:T(1,128)S(1)}, f32[1,256]{1,0:T(1,128)},...) fusion(f32[16,256]{1,0:T(8,128)} %param.8), kind=kLoop, calls=%fused_computation.141 | loop fusion | bytes 32768 | tf_op jit(solution)/shard_map/slice | solution.py:27
  5.0 3.5 %copy.96 = bf16[2,128,5888]{1,2,0:T(8,128)(2,1)S(1)} copy(bf16[2,128,5888]{2,1,0:T(8,128)(2,1)} %param.7) | data formatting | bytes 6029312 | tf_op args[0]
  8.5 1.1 maximum_bitcast_fusion.1
  9.6 7.1 %bitcast_convert_fusion = bf16[256,2,128,8]{2,0,3,1:T(8,128)(2,1)S(1)} fusion(bf16[2,128,23,256]{1,3,2,0:T(8,128)(2,1)S(1)} %bitcast.122, f32[256,1,2,256]{3,0,2,1:T(8,128)S(1)} %get-tuple-element.26, f32[256,1,2,256]{3,0,2,1:T(8,128)S(1)} %get-tuple-element.25, f32[256]{0:T(256)} %bitcast.145, f32[256]{0:T(256)} %bitcast.146, f32[256]{0:T(256)S(1)} %bitcast.132, ...), kind=kOutput, calls=%fused_computation.10 | convolution fusion | flops 3246653440 | bytes 18890752 | tf_op jit(solution)/shard_map/crsk,sitk->crit/dot_general | solution.py:30
  16.7 1.6 %copy.98 = bf16[256,2,128,8]{2,3,1,0:T(8,128)(2,1)} copy(bf16[256,2,128,8]{2,0,3,1:T(8,128)(2,1)S(1)} %bitcast_convert_fusion) | data formatting | bytes 2097152 | tf_op jit(solution)/shard_map/convert_element_type | solution.py:37
  18.4 7.4 %all-to-all-start = ((bf16[256,2,128,8]{2,3,1,0:T(8,128)(2,1)}), bf16[256,2,128,8]{2,3,1,0:T(8,128)(2,1)S(1)}, u32[]{:S(2)}, u32[]{:S(2)}) async-start(bf16[256,2,128,8]{2,3,1,0:T(8,128)(2,1)} %copy.98), calls=%async_computation | async-start | bytes 2097152 | tf_op jit(solution)/shard_map/all_to_all | solution.py:72
  26.2 25.3 %all-to-all-done = bf16[256,2,128,8]{2,3,1,0:T(8,128)(2,1)S(1)} async-done(((bf16[256,2,128,8]{2,3,1,0:T(8,128)(2,1)}), bf16[256,2,128,8]{2,3,1,0:T(8,128)(2,1)S(1)}, u32[]{:S(2)}, u32[]{:S(2)}) %all-to-all-start) | async-done | bytes 1048608 | tf_op jit(solution)/shard_map/all_to_all | solution.py:72
  51.5 0.3 copy.144
  51.8 6.9 %fusion.58 = f32[32,2,2,64,2]{3,4,1,2,0:T(2,128)S(1)} fusion(bf16[32,2,1024,8]{2,3,1,0:T(8,128)(2,1)S(1)} %bitcast.118, s32[]{:T(128)S(6)} %select_n.39, bf16[2,32,64,1024]{3,2,1,0:T(8,128)(2,1)} %param.9, bf16[64,1024]{1,0:T(8,128)(2,1)S(1)} %copy.104), kind=kOutput, calls=%fused_computation.64 | convolution fusion | flops 37748736 | bytes 8847364 | tf_op jit(solution)/shard_map/scbi,crit->csrbt/dot_general | solution.py:59
  58.9 0.7 reshape.184
  59.7 3.3 %all-to-all-start.1 = ((bf16[4,2,1024]{2,1,0:T(2,128)(2,1)}), bf16[4,2,1024]{2,1,0:T(2,128)(2,1)S(1)}, u32[]{:S(2)}, u32[]{:S(2)}) async-start(bf16[4,2,1024]{2,1,0:T(2,128)(2,1)} %reshape.184), calls=%async_computation.1 | async-start | bytes 32768 | tf_op jit(solution)/shard_map/all_to_all | solution.py:78
  62.9 1.0 gather_fusion.1
  63.9 1.2 fusion.97
  65.1 0.2 fusion.118
  65.3 0.2 maximum_bitcast_fusion
  65.5 1.0 gather_fusion
  66.5 0.2 all-to-all-done.1
  66.9 0.7 reshape.186
  67.6 3.6 %all-to-all-start.2 = ((bf16[8,2,512]{2,1,0:T(2,128)(2,1)}), bf16[8,2,512]{2,1,0:T(2,128)(2,1)S(1)}, u32[]{:S(2)}, u32[]{:S(2)}) async-start(bf16[8,2,512]{2,1,0:T(2,128)(2,1)} %reshape.186), calls=%async_computation.2 | async-start | bytes 32768 | tf_op jit(solution)/shard_map/all_to_all | solution.py:77
  71.2 16.0 %fusion = f32[2,32,9,128,128]{3,4,0,2,1:T(8,128)} fusion(bf16[1,32,2,9,128,8]{4,5,2,0,3,1:T(8,128)(2,1)S(1)} %maximum_bitcast_fusion, bf16[1,32,2,9,128,8]{4,5,2,0,3,1:T(8,128)(2,1)} %get-tuple-element.19, bf16[9,32,2,128,8]{3,4,2,1,0:T(8,128)(2,1)S(1)} %gather_fusion, pred[9]{0:T(512)(128)(4,1)S(1)} %get-tuple-element.15), kind=kOutput, calls=%fused_computation.3 | convolution fusion | flops 316735488 | bytes 41287688 | tf_op jit(solution)/shard_map/ocrkaw,crkbw->ockab/dot_general | solution.py:49
  87.2 36.9 %copy.113 = f32[2,32,9,128,128]{4,3,2,1,0:T(8,128)} copy(f32[2,32,9,128,128]{3,4,0,2,1:T(8,128)} %fusion) | data formatting | bytes 75497472
  124.2 0.7 all_to_all.44
  (21 shorter events, 0.9 us)
Async XLA Ops:
  16.7 9.1 %copy-start = (s32[64,512]{1,0:T(8,128)S(1)}, s32[64,512]{1,0:T(8,128)}, u32[]{:S(2)}) copy-start(s32[64,512]{1,0:T(8,128)} %param.10) | copy-start | bytes 393220
  18.4 7.8 %copy-start.1 = (s32[9,2]{0,1:T(2,128)S(1)}, s32[9,2]{0,1:T(2,128)}, u32[]{:S(2)}) copy-start(s32[9,2]{0,1:T(2,128)} %param.11) | copy-start | bytes 220
  18.4 33.2 %all-to-all-start = ((bf16[256,2,128,8]{2,3,1,0:T(8,128)(2,1)}), bf16[256,2,128,8]{2,3,1,0:T(8,128)(2,1)S(1)}, u32[]{:S(2)}, u32[]{:S(2)}) async-start(bf16[256,2,128,8]{2,3,1,0:T(8,128)(2,1)} %copy.98), calls=%async_computation | async-start | bytes 2097152 | tf_op jit(solution)/shard_map/all_to_all | solution.py:72
  59.7 7.1 %all-to-all-start.1 = ((bf16[4,2,1024]{2,1,0:T(2,128)(2,1)}), bf16[4,2,1024]{2,1,0:T(2,128)(2,1)S(1)}, u32[]{:S(2)}, u32[]{:S(2)}) async-start(bf16[4,2,1024]{2,1,0:T(2,128)(2,1)} %reshape.184), calls=%async_computation.1 | async-start | bytes 32768 | tf_op jit(solution)/shard_map/all_to_all | solution.py:78
  67.6 56.5 %all-to-all-start.2 = ((bf16[8,2,512]{2,1,0:T(2,128)(2,1)}), bf16[8,2,512]{2,1,0:T(2,128)(2,1)S(1)}, u32[]{:S(2)}, u32[]{:S(2)}) async-start(bf16[8,2,512]{2,1,0:T(2,128)(2,1)} %reshape.186), calls=%async_computation.2 | async-start | bytes 32768 | tf_op jit(solution)/shard_map/all_to_all | solution.py:77
where the time goes:
time: 126 us; the launch traced here: 125 us
  local copies, waits for them, and re-layouts  48.9 us (39%)
  matrix products  29.9 us (24%)
  waiting for transfers between devices  25.5 us (20%)
  starting transfers between devices  14.2 us (11%)
  other arithmetic  5.54 us (4%)
    unnamed x10, local copies, waits for them, and re-layouts  42 us
    all_to_all x1, waiting for transfers between devices, on_device(): lax.all_to_all(spectra, 'chan', split_axis=0, concat_axis=2, tiled=True)  25.3 us
    dot_general x1, matrix products, correlate(): jnp.einsum('ocrkaw,crkbw->ockab', stacked, right_rows, preferred_element_...  16 us
    all_to_all x1, starting transfers between devices, on_device(): lax.all_to_all(spectra, 'chan', split_axis=0, concat_axis=2, tiled=True)  7.38 us
    dot_general x1, matrix products, filterbank(): jnp.einsum('crsk,sitk->crit', dft_table(channels), frames, precision=lax....  7.12 us
    dot_general x1, matrix products, beamform(): jnp.einsum('scbi,crit->csrbt', weights, own_time, preferred_element_type=...  6.86 us
    all_to_all x1, starting transfers between devices, on_device(): lax.all_to_all(lax.all_to_all(beam_part, 'tile', split_axis=1, concat_axi...  3.59 us
    all_to_all x1, starting transfers between devices, on_device(): lax.all_to_all(beam_part, 'tile', split_axis=1, concat_axis=2, tiled=True)  3.25 us
  transfers between devices with their start and end apart: 3, of which 2 were waited for; matrix products, arithmetic and copies ran while one was open for 46% of the time, Pallas kernels for 0%

commit v1 on v0

--- a/solution.py
+++ b/solution.py
@@ -69,7 +69,10 @@
     quarter = total_time // tile_count
     tile_index = lax.axis_index("tile")
     spectra = filterbank(voltages, taps, total_time)
-    turned = lax.all_to_all(spectra, "chan", split_axis=0, concat_axis=2, tiled=True)
+    devices = lax.axis_size("chan")
+    tiles = jnp.stack(jnp.split(spectra, devices, axis=0), axis=0)
+    tiles = lax.all_to_all(tiles, "chan", split_axis=0, concat_axis=0)
+    turned = jnp.concatenate(tiles, axis=2)
     own_time = lax.dynamic_slice_in_dim(turned, tile_index * quarter, quarter, 3)
     visibility = correlate(turned, tile_pairs)
     visibility = visibility * (1.0 / total_time)

time: 126 us -> 131 us (1.040)
  local copies, waits for them, and re-layouts: 48.9 us -> 55.5 us
    unnamed x10 -> x21, local copies, waits for them, and re-layouts: 42 us -> 48.4 us
    convert_element_type x1 -> x0, local copies, waits for them, and re-layouts: 1.65 us -> none  [filterbank(): return spectra.astype(jnp.bfloat16)]
    all_to_all x3, local copies, waits for them, and re-layouts: 0.02 us -> 1.49 us  [on_device(): lax.all_to_all(beam_part, 'tile', split_axis=1, concat_axis=2, tiled=True)]
  transfers between devices with their start and end apart: 3 -> 3, of which waited for: 2 -> 2; matrix products, arithmetic and copies ran while one was open for 46% -> 43% of each run, Pallas kernels for 0% -> 0%
where the time goes in v1:
time: 131 us; the launch traced here: 130 us
  local copies, waits for them, and re-layouts  55.5 us (42%)
  matrix products  28.7 us (22%)
  waiting for transfers between devices  25.1 us (19%)
  starting transfers between devices  14.1 us (11%)
  other arithmetic  5.99 us (5%)
    unnamed x21, local copies, waits for them, and re-layouts  48.4 us
    all_to_all x1, waiting for transfers between devices, on_device(): tiles = lax.all_to_all(tiles, 'chan', split_axis=0, concat_axis=0)  24.1 us
    dot_general x1, matrix products, correlate(): jnp.einsum('ocrkaw,crkbw->ockab', stacked, right_rows, preferred_element_...  14.8 us
    all_to_all x1, starting transfers between devices, on_device(): tiles = lax.all_to_all(tiles, 'chan', split_axis=0, concat_axis=0)  7.26 us
    dot_general x1, matrix products, filterbank(): jnp.einsum('crsk,sitk->crit', dft_table(channels), frames, precision=lax....  7.13 us
    dot_general x1, matrix products, beamform(): jnp.einsum('scbi,crit->csrbt', weights, own_time, preferred_element_type=...  6.84 us
    all_to_all x1, starting transfers between devices, on_device(): lax.all_to_all(lax.all_to_all(beam_part, 'tile', split_axis=1, concat_axi...  3.59 us
    all_to_all x1, starting transfers between devices, on_device(): lax.all_to_all(beam_part, 'tile', split_axis=1, concat_axis=2, tiled=True)  3.25 us
  transfers between devices with their start and end apart: 3, of which 2 were waited for; matrix products, arithmetic and copies ran while one was open for 43% of the time, Pallas kernels for 0%

profile of v1, /device:TPU:0, one launch (start us, length us, event | category | flops | bytes accessed | tf_op | source)
XLA Modules:
  0.0 130.3 jit_solution(9184726608319622639)
XLA Ops:
  0.6 1.0 fusion.115
  1.6 1.7 %fusion.113 = (f32[256,1,256]{2,0,1:T(8,128)S(1)}, f32[256,1,256]{2,0,1:T(8,128)}) fusion(), kind=kLoop, calls=%fused_computation.133 | loop fusion | flops 917504 | bytes 524288 | tf_op jit(solution)/shard_map/sin | solution.py:15
  3.3 1.7 %fusion.124 = (f32[1,256]{1,0:T(1,128)S(1)}, f32[1,256]{1,0:T(1,128)S(1)}, f32[1,256]{1,0:T(1,128)S(1)}, f32[1,256]{1,0:T(1,128)S(1)}, f32[1,256]{1,0:T(1,128)},...) fusion(f32[16,256]{1,0:T(8,128)} %param.8), kind=kLoop, calls=%fused_computation.154 | loop fusion | bytes 32768 | tf_op jit(solution)/shard_map/slice | solution.py:27
  5.0 3.5 %copy.74 = bf16[2,128,5888]{1,2,0:T(8,128)(2,1)S(1)} copy(bf16[2,128,5888]{2,1,0:T(8,128)(2,1)} %param.7) | data formatting | bytes 6029312 | tf_op args[0]
  8.5 1.1 maximum_bitcast_fusion.1
  9.6 7.1 %bitcast_convert_fusion = bf16[256,2,128,8]{2,0,3,1:T(8,128)(2,1)S(1)} fusion(bf16[2,128,23,256]{1,3,2,0:T(8,128)(2,1)S(1)} %bitcast.146, f32[256,1,2,256]{3,0,2,1:T(8,128)S(1)} %get-tuple-element.22, f32[256,1,2,256]{3,0,2,1:T(8,128)S(1)} %get-tuple-element.21, f32[256]{0:T(256)} %bitcast.170, f32[256]{0:T(256)} %bitcast.171, f32[256]{0:T(256)S(1)} %bitcast.157, ...), kind=kOutput, calls=%fused_computation.9 | convolution fusion | flops 3246653440 | bytes 18890752 | tf_op jit(solution)/shard_map/crsk,sitk->crit/dot_general | solution.py:30
  16.8 0.7 fusion.112
  17.4 0.7 fusion.111
  20.7 0.7 fusion.106
  22.1 7.3 %all-to-all-start = ((bf16[8,32,2,128,8]{3,1,4,2,0:T(8,128)(2,1)}), bf16[8,32,2,128,8]{3,1,4,2,0:T(8,128)(2,1)S(1)}, u32[]{:S(2)}, u32[]{:S(2)}) async-start(bf16[8,32,2,128,8]{3,1,4,2,0:T(8,128)(2,1)} %fusion.105), calls=%async_computation | async-start | bytes 2097152 | tf_op jit(solution)/shard_map/all_to_all | solution.py:74
  31.0 24.1 %all-to-all-done = bf16[8,32,2,128,8]{3,1,4,2,0:T(8,128)(2,1)S(1)} async-done(((bf16[8,32,2,128,8]{3,1,4,2,0:T(8,128)(2,1)}), bf16[8,32,2,128,8]{3,1,4,2,0:T(8,128)(2,1)S(1)}, u32[]{:S(2)}, u32[]{:S(2)}) %all-to-all-start) | async-done | bytes 1048608 | tf_op jit(solution)/shard_map/all_to_all | solution.py:74
  55.5 6.8 %fusion.56 = f32[32,2,2,64,2]{3,4,1,2,0:T(2,128)S(1)} fusion(bf16[32,2,1024,8]{2,3,1,0:T(8,128)(2,1)S(1)} %bitcast.148, s32[]{:T(128)S(6)} %select_n.39, bf16[2,32,64,1024]{3,2,1,0:T(8,128)(2,1)} %param.9, bf16[64,1024]{1,0:T(8,128)(2,1)S(1)} %copy.80), kind=kOutput, calls=%fused_computation.63 | convolution fusion | flops 37748736 | bytes 8847364 | tf_op jit(solution)/shard_map/scbi,crit->csrbt/dot_general | solution.py:59
  62.6 0.7 reshape.190
  63.3 3.3 %all-to-all-start.1 = ((bf16[4,2,1024]{2,1,0:T(2,128)(2,1)}), bf16[4,2,1024]{2,1,0:T(2,128)(2,1)S(1)}, u32[]{:S(2)}, u32[]{:S(2)}) async-start(bf16[4,2,1024]{2,1,0:T(2,128)(2,1)} %reshape.190), calls=%async_computation.1 | async-start | bytes 32768 | tf_op jit(solution)/shard_map/all_to_all | solution.py:81
  66.6 0.8 gather_fusion.1
  67.4 0.9 gather_fusion
  69.4 1.0 all-to-all-done.1
  70.4 0.7 reshape.191
  71.1 0.8 copy.85
  72.6 1.6 %reshape.192 = bf16[8,2,512]{2,1,0:T(2,128)(2,1)} reshape(bf16[8,2,16,32]{3,2,1,0:T(8,128)(2,1)} %bitcast.151) | data formatting | bytes 32768
  74.2 3.6 %all-to-all-start.2 = ((bf16[8,2,512]{2,1,0:T(2,128)(2,1)}), bf16[8,2,512]{2,1,0:T(2,128)(2,1)S(1)}, u32[]{:S(2)}, u32[]{:S(2)}) async-start(bf16[8,2,512]{2,1,0:T(2,128)(2,1)} %reshape.192), calls=%async_computation.2 | async-start | bytes 32768 | tf_op jit(solution)/shard_map/all_to_all | solution.py:80
  77.8 14.8 %fusion = f32[2,32,9,128,128]{3,4,0,2,1:T(8,128)} fusion(bf16[2,32,2,9,128,8]{4,1,5,2,3,0:T(8,128)(2,1)S(1)} %pad_maximum_fusion, bf16[32,2,9,128,8,1]{3,0,4,1,2,5:T(8,128)(2,1)S(1)} %select_bitcast_fusion), kind=kOutput, calls=%fused_computation.3 | convolution fusion | flops 311427072 | bytes 41287680 | tf_op jit(solution)/shard_map/ocrkaw,crkbw->ockab/dot_general | solution.py:49
  92.6 36.9 %copy.89 = f32[2,32,9,128,128]{4,3,2,1,0:T(8,128)} copy(f32[2,32,9,128,128]{3,4,0,2,1:T(8,128)} %fusion) | data formatting | bytes 75497472
  129.6 0.7 all_to_all.31
  (34 shorter events, 7.4 us)
Async XLA Ops:
  16.7 12.6 %copy-start = (s32[64,512]{1,0:T(8,128)S(1)}, s32[64,512]{1,0:T(8,128)}, u32[]{:S(2)}) copy-start(s32[64,512]{1,0:T(8,128)} %param.10) | copy-start | bytes 393220
  20.1 9.7 %copy-start.3 = (s32[9,2]{0,1:T(2,128)S(1)}, s32[9,2]{0,1:T(2,128)}, u32[]{:S(2)}) copy-start(s32[9,2]{0,1:T(2,128)} %param.11) | copy-start | bytes 220
  22.1 33.0 %all-to-all-start = ((bf16[8,32,2,128,8]{3,1,4,2,0:T(8,128)(2,1)}), bf16[8,32,2,128,8]{3,1,4,2,0:T(8,128)(2,1)S(1)}, u32[]{:S(2)}, u32[]{:S(2)}) async-start(bf16[8,32,2,128,8]{3,1,4,2,0:T(8,128)(2,1)} %fusion.105), calls=%async_computation | async-start | bytes 2097152 | tf_op jit(solution)/shard_map/all_to_all | solution.py:74
  63.3 7.1 %all-to-all-start.1 = ((bf16[4,2,1024]{2,1,0:T(2,128)(2,1)}), bf16[4,2,1024]{2,1,0:T(2,128)(2,1)S(1)}, u32[]{:S(2)}, u32[]{:S(2)}) async-start(bf16[4,2,1024]{2,1,0:T(2,128)(2,1)} %reshape.190), calls=%async_computation.1 | async-start | bytes 32768 | tf_op jit(solution)/shard_map/all_to_all | solution.py:81
  67.3 0.9 copy-start.2
  68.3 0.6 copy-start.1
  74.2 55.3 %all-to-all-start.2 = ((bf16[8,2,512]{2,1,0:T(2,128)(2,1)}), bf16[8,2,512]{2,1,0:T(2,128)(2,1)S(1)}, u32[]{:S(2)}, u32[]{:S(2)}) async-start(bf16[8,2,512]{2,1,0:T(2,128)(2,1)} %reshape.192), calls=%async_computation.2 | async-start | bytes 32768 | tf_op jit(solution)/shard_map/all_to_all | solution.py:80
